TPU v7x, 256 devices: a whole 4x4x8 slice. The times are simulated.
256 devices in a mesh: chan: 16 (over y, x), row: 4 (over z_lo), col: 4 (over z_hi, core).
Axes of the slice: x: 4, y: 4, z: 8 (z_hi: 2, z_lo: 4; z = z_hi * 4 + z_lo), core: 2. Of those that a mesh axis runs over, the one named last changes fastest.
Arguments:
- voltages: bfloat16 [2, 2048, 265216], P(None, ('row', 'col', 'chan')), may hold values from -6 to 6
- fir_window: float32 [4, 1024], replicated, may hold values from 0.5 to 1.5
- flags: int32 [2048, 256], P(('row', 'col', 'chan')), may hold values 0 or 1
Outputs:
- visibility: float32 [2, 32, 2048, 4, 512], P(None, 'chan', 'row', None, 'col')
All inputs are finite; a program needn't handle non-finite values. No bound on the sum of `flags` on one device may be relied on, other than what follows from the above.
Results may differ from a plain program's by a relative error of at most 0.0039.
Values may be sent and summed in bfloat16 or wider, within the bound.
A program may use at most 128 MiB of HBM per device.

v0:
```python
import math

import jax
import jax.numpy as jnp
from jax import lax
from jax.sharding import PartitionSpec as P

CHANNEL_COUNT = 1024
FILTER_TAPS = 4
CH_DEV = 2


def build_table(fir_window, band_total):
    chan_index = jnp.arange(CHANNEL_COUNT, dtype=jnp.int32)
    band_index = jnp.arange(band_total, dtype=jnp.int32)
    phase_index = chan_index[:, None] * band_index[None, :] % CHANNEL_COUNT
    angles = phase_index.astype(jnp.float32) * (2.0 * math.pi / CHANNEL_COUNT)
    weighting = fir_window / math.sqrt(FILTER_TAPS * CHANNEL_COUNT)
    cosine = (weighting[:, :, None] * jnp.cos(angles)[None]).astype(jnp.bfloat16)
    sine_part = (weighting[:, :, None] * jnp.sin(angles)[None]).astype(jnp.bfloat16)
    real_input = jnp.stack([cosine, -sine_part], axis=2)
    imag_input = jnp.stack([sine_part, cosine], axis=2)
    return jnp.stack([real_input, imag_input], axis=0)


def product(first_half, second_half):
    return jnp.einsum("kas,kbs->kab", first_half, second_half, preferred_element_type=jnp.float32)


def cross_power(first_set, second_set):
    spectra_total = first_set.shape[-1]
    real_part = product(first_set[0], second_set[0]) + product(first_set[1], second_set[1])
    imag_part = product(first_set[1], second_set[0]) - product(first_set[0], second_set[1])
    return jnp.stack([real_part, imag_part]) * (1.0 / math.sqrt(spectra_total))


def on_device(voltages, fir_window, flags):
    antenna_total = voltages.shape[1]
    spectra_total = flags.shape[1]
    band_total = CH_DEV * lax.axis_size("chan")
    coef_table = build_table(fir_window, band_total)
    filter_frames = voltages.reshape(
        2, antenna_total, spectra_total + FILTER_TAPS - 1, CHANNEL_COUNT
    )
    summed_power = jnp.zeros((2, band_total, antenna_total, spectra_total), jnp.float32)
    for tap in range(FILTER_TAPS):
        summed_power = summed_power + jnp.einsum(
            "pasn,pnqk->qkas",
            filter_frames[:, :, tap : tap + spectra_total],
            coef_table[:, tap],
            preferred_element_type=jnp.float32,
        )
    spectra_rows = (summed_power * flags.astype(jnp.float32)[None, None]).astype(jnp.bfloat16)
    turned = lax.all_to_all(spectra_rows, "chan", split_axis=1, concat_axis=2, tiled=True)
    group_chans = turned.shape[1]
    sub_count = turned.shape[2]
    row_count = lax.axis_size("row")
    col_count = lax.axis_size("col")
    gathered = lax.all_gather(turned, ("row", "col"), axis=2, tiled=True)
    grid = gathered.reshape(2, group_chans, row_count, col_count, sub_count, spectra_total)
    row_block = lax.dynamic_index_in_dim(grid, lax.axis_index("row"), 2, keepdims=False)
    row_block = row_block.reshape(2, group_chans, col_count * sub_count, spectra_total)
    column_set = lax.dynamic_index_in_dim(grid, lax.axis_index("col"), 3, keepdims=False)
    column_set = column_set.reshape(2, group_chans, row_count * sub_count, spectra_total)
    visibility = cross_power(row_block, column_set)
    return visibility.reshape(
        2, group_chans, visibility.shape[2], row_count, visibility.shape[3] // row_count
    )


def solution(mesh):
    return jax.shard_map(
        on_device,
        mesh=mesh,
        in_specs=(P(None, ("row", "col", "chan"), None), P(), P(("row", "col", "chan"), None)),
        out_specs=P(None, "chan", "row", None, "col"),
        check_vma=False,
    )
```

profile of v0, /device:TPU:1, one launch (start us, length us, event | category | flops | bytes accessed | tf_op | source)
XLA Modules:
  0.0 220.9 jit_solution(6056581019566765027)
XLA Ops:
  6.5 0.0 all-gather.2.cloned.1.call-start
  6.5 0.5 fusion.31
  7.1 0.7 broadcast_multiply_fusion
  7.8 0.1 multiply_convert_fusion
  7.9 0.0 copy-start.1
  7.9 17.2 %fusion.38 = (bf16[2,8,256,1024]{3,1,2,0:T(8,128)(2,1)S(1)}, bf16[2,8,256,1024]{3,1,2,0:T(8,128)(2,1)S(1)}, bf16[2,8,256,1024]{3,1,2,0:T(8,128)(2,1)}, bf16[2,8,256,1024]{3,1,2,0:T(8,128)(2,1)}) fusion(bf16[2,8,259,1024]{3,1,2,0:T(8,128)(2,1)} %bitcast.104), kind=kLoop, calls=%fused_computation.61 | loop fusion | bytes 67108864 | tf_op jit(solution)/shard_map/slice | solution.py:49
  25.2 0.0 copy-done.1
  25.2 0.0 copy-start
  25.2 0.1 maximum_bitcast_fusion.1
  25.3 8.4 %fusion.4 = f32[2,32,8,256]{3,1,2,0:T(8,128)S(1)} fusion(bf16[2,8,256,1024]{3,1,2,0:T(8,128)(2,1)} %get-tuple-element.8, bf16[1,4,1024,2,32]{2,4,0,3,1:T(8,128)(2,1)S(1)} %get-tuple-element.14, bf16[1,4,1024,2,32]{2,4,0,3,1:T(8,128)(2,1)S(1)} %get-tuple-element.13), kind=kOutput, calls=%fused_computation.17 | convolution fusion | flops 537395200 | bytes 9961472 | tf_op jit(solution)/shard_map/pasn,pnqk->qkas/dot_general | solution.py:47
  33.7 0.0 copy-done
  33.7 4.9 %fusion.11 = f32[2,32,8,256]{3,1,2,0:T(8,128)S(1)} fusion(f32[2,32,8,256]{3,1,2,0:T(8,128)S(1)} %fusion.4, bf16[2,8,256,1024]{3,1,2,0:T(8,128)(2,1)S(1)} %copy-done, bf16[1,4,1024,2,32]{2,4,0,3,1:T(8,128)(2,1)S(1)} %get-tuple-element.14, bf16[1,4,1024,2,32]{2,4,0,3,1:T(8,128)(2,1)S(1)} %get-tuple-element.13), kind=kOutput, calls=%fused_computation.24 | convolution fusion | flops 537526272 | bytes 10485760 | tf_op jit(solution)/shard_map/pasn,pnqk->qkas/dot_general | solution.py:47
  38.6 5.1 %fusion.10 = f32[2,32,8,256]{3,1,2,0:T(8,128)S(1)} fusion(f32[2,32,8,256]{3,1,2,0:T(8,128)S(1)} %fusion.11, bf16[2,8,256,1024]{3,1,2,0:T(8,128)(2,1)S(1)} %get-tuple-element.6, bf16[1,4,1024,2,32]{2,4,0,3,1:T(8,128)(2,1)S(1)} %get-tuple-element.14, bf16[1,4,1024,2,32]{2,4,0,3,1:T(8,128)(2,1)S(1)} %get-tuple-element.13), kind=kOutput, calls=%fused_computation.23 | convolution fusion | flops 537526272 | bytes 10485760 | tf_op jit(solution)/shard_map/pasn,pnqk->qkas/dot_general | solution.py:47
  43.7 4.9 %fusion.12 = bf16[2,32,8,256]{3,1,2,0:T(8,128)(2,1)S(1)} fusion(f32[2,32,8,256]{3,1,2,0:T(8,128)S(1)} %fusion.10, bf16[2,8,256,1024]{3,1,2,0:T(8,128)(2,1)S(1)} %get-tuple-element.5, bf16[1,4,1024,2,32]{2,4,0,3,1:T(8,128)(2,1)S(1)} %get-tuple-element.13, bf16[1,4,1024,2,32]{2,4,0,3,1:T(8,128)(2,1)S(1)} %get-tuple-element.14, ...), kind=kOutput, calls=%fused_computation.25 | convolution fusion | flops 537788416 | bytes 10231808 | tf_op jit(solution)/shard_map/pasn,pnqk->qkas/dot_general | solution.py:47
  48.6 0.2 copy.31
  48.8 14.9 %all_to_all.18 = bf16[2,32,8,256]{3,2,0,1:T(8,128)(2,1)S(1)} all-to-all(bf16[2,32,8,256]{3,2,0,1:T(8,128)(2,1)S(1)} %copy.31), channel_id=1, replica_groups=mesh['chan'=16,'row'=4,'col'=4] {'chan'}, dimensions={1} | all-to-all | bytes 524288 | tf_op jit(solution)/shard_map/all_to_all | solution.py:54
  63.7 0.7 copy.76
  64.4 0.0 all-gather.2.cloned.1.call-update
  64.4 132.9 %all-gather.2.cloned.1.call-done = bf16[2,2,2048,256]{3,2,1,0:T(8,128)(2,1)} async-done(((bf16[2,2,128,256]{3,2,1,0:T(8,128)(2,1)}), bf16[2,2,2048,256]{3,2,1,0:T(8,128)(2,1)}) %all-gather.2.cloned.1.call-update) | async-done | bytes 4194320 | tf_op jit(solution)/shard_map/all_gather | solution.py:59
  197.3 1.3 constant_dynamic-slice_fusion.2
  198.6 1.3 constant_dynamic-slice_fusion.1
  199.9 0.5 fusion.39
  200.3 0.5 fusion.40
  200.8 1.8 convolution_add_fusion
  202.6 2.9 %copy.34 = f32[1,2,512,4,128]{4,3,2,1,0:T(4,128)} copy(f32[1,2,512,4,128]{2,4,3,1,0:T(8,128)} %bitcast.106) | data formatting | bytes 4194304 | tf_op jit(solution)/shard_map/stack | solution.py:34
  205.5 1.8 convolution_subtract_fusion
  207.3 2.0 copy.35
  209.4 4.7 %maximum_multiply_fusion = f32[2,2,512,4,128]{4,3,2,1,0:T(4,128)} fusion(f32[1,2,512,4,128]{4,3,2,1,0:T(4,128)S(1)} %copy.35, f32[1,2,512,4,128]{4,3,2,1,0:T(4,128)} %copy.34), kind=kLoop, calls=%fused_computation.8 | loop fusion | flops 2097152 | bytes 8388608 | tf_op jit(solution)/shard_map/mul | solution.py:34
  (2 shorter events, 0.1 us)
Async XLA Ops:
  6.5 190.8 %all-gather.2.cloned.1.call-start = ((), (), s32[]{:S(2)}) async-start(), calls=%async_computation.1 | async-start | bytes 4456448 | tf_op jit(solution)/shard_map/all_gather | solution.py:59
  7.9 17.3 %copy-start.1 = (s32[8,256]{1,0:T(8,128)S(1)}, s32[8,256]{1,0:T(8,128)}, u32[]{:S(2)}) copy-start(s32[8,256]{1,0:T(8,128)} %param.5) | copy-start | bytes 24580
  25.2 8.5 %copy-start = (bf16[2,8,256,1024]{3,1,2,0:T(8,128)(2,1)S(1)}, bf16[2,8,256,1024]{3,1,2,0:T(8,128)(2,1)}, u32[]{:S(2)}) copy-start(bf16[2,8,256,1024]{3,1,2,0:T(8,128)(2,1)} %get-tuple-element.7) | copy-start | bytes 25165828
Sparse Core Ops, SparseCore 0:
  64.6 132.6 all-gather.1
where the time goes:
time: 221 us
  waiting for transfers between devices  133 us (60%)
  matrix products  27.8 us (13%)
  local copies, waits for them, and re-layouts  25.6 us (12%)
  blocking collectives  14.9 us (7%)
  between operations  13.5 us (6%)
  other arithmetic  6.14 us (3%)
    all_gather x1, waiting for transfers between devices, on_device(): gathered = lax.all_gather(turned, ('row', 'col'), axis=2, tiled=True)  133 us
    dot_general x4, matrix products, on_device(): jnp.einsum('pasn,pnqk->qkas', filter_frames[:, :, tap:tap + spectra_total...  23.3 us
    slice x1, local copies, waits for them, and re-layouts, on_device(): filter_frames[:, :, tap:tap + spectra_total]  17.2 us
    all_to_all x1, blocking collectives, on_device(): lax.all_to_all(spectra_rows, 'chan', split_axis=1, concat_axis=2, tiled=T...  14.9 us
    another operation x2, local copies, waits for them, and re-layouts, cross_power(): return jnp.stack([real_part, imag_part]) * (1.0 / math.sqrt(spectra_total))  4.95 us
    mul x1, other arithmetic, cross_power(): return jnp.stack([real_part, imag_part]) * (1.0 / math.sqrt(spectra_total))  4.68 us
    dot_general x4, matrix products, product(): jnp.einsum('kas,kbs->kab', first_half, second_half, preferred_element_typ...  4.54 us
  transfers between devices with their start and end apart: 1, of which 1 were waited for; matrix products, arithmetic and copies ran while one was open for 0% of the time, Pallas kernels for 0%

commit v1 on v0

v1 whole, which is shorter than its diff:
```python
import functools
import math

import jax
import jax.numpy as jnp
import numpy as np
from jax import lax
from jax.experimental import pallas as pl
from jax.experimental.pallas import tpu as pltpu
from jax.sharding import PartitionSpec as P

MESH = pl.DeviceIdType.MESH

CHANNELS = 1024
TAPS = 4
BAND = 32
SPECTRA = 256
FRAMES = SPECTRA + TAPS - 1
ANT = 8
GROUPS = 16
PER = BAND // GROUPS
N_ROW = 4
PLANES = 8
CHUNKS = 2
WIDTH = SPECTRA // CHUNKS
BOUNDS = (0, 132, FRAMES)
BLOCK = 44
PADDED = 264

PLAN = {
    0: [(0, 0, 1, False), (0, 3, -1, True), (0, 2, -2, True), (1, 0, 1, False), (1, 3, -1, True), (1, 2, -2, True)],
    1: [
        (0, 1, 1, False), (0, 1, -1, False), (0, 0, 1, False), (0, 2, -1, False), (0, 3, -1, False),
        (1, 1, 1, False), (1, 1, -1, False), (1, 0, 1, False), (1, 2, -1, False), (1, 3, -1, False),
    ],
    2: [
        (0, 2, -1, False), (0, 2, 1, False), (0, 3, -1, False), (0, 1, 1, False), (0, 0, 1, False),
        (1, 2, -1, False), (1, 2, 1, False), (1, 3, -1, False), (1, 1, 1, False), (1, 0, 1, False),
    ],
    3: [(0, 3, -1, False), (0, 0, 1, True), (0, 1, 2, True), (1, 3, -1, False), (1, 0, 1, True), (1, 1, 2, True)],
}


def basis():
    n = np.arange(CHANNELS)[:, None]
    k = np.arange(BAND)[None, :]
    angle = ((n * k) % CHANNELS).astype(np.float32) * np.float32(2.0 * math.pi / CHANNELS)
    cos, sin = np.cos(angle), np.sin(angle)
    return np.stack([np.concatenate([cos, -sin], 1), np.concatenate([sin, cos], 1)])


def gather_kernel(
    volt, table, flags, rows, cols,
    vbuf, gbuf, cbuf, tbuf, sbuf,
    volt_sem, turn_send, turn_recv, own_sem, line_send, row_recv, col_recv, swap_send,
):
    k = lax.axis_index("chan")
    r = lax.axis_index("row")
    c = lax.axis_index("col")
    hi, core = c // 2, c % 2
    plane = hi * N_ROW + r
    other = 1 - core

    def at_plane(offset):
        z = (plane + offset + PLANES) % PLANES
        return (k, z % N_ROW, (z // N_ROW) * 2 + core)

    mate = (k, r, hi * 2 + other)

    reads = []
    for chunk in range(CHUNKS):
        lo, up = BOUNDS[chunk], BOUNDS[chunk + 1]
        copy = pltpu.make_async_copy(
            volt.at[:, pl.ds(lo, up - lo)], vbuf.at[:, pl.ds(lo, up - lo)], volt_sem.at[chunk]
        )
        copy.start()
        reads.append(copy)

    barrier = pltpu.get_barrier_semaphore()

    def greet(d, carry):
        pl.semaphore_signal(barrier, inc=1, device_id=((k + d) % GROUPS, r, c), device_id_type=MESH)
        return carry

    lax.fori_loop(1, GROUPS, greet, 0)
    for offset in (-2, -1, 1, 2):
        pl.semaphore_signal(barrier, inc=1, device_id=at_plane(offset), device_id_type=MESH)
    pl.semaphore_signal(barrier, inc=1, device_id=mate, device_id_type=MESH)

    def channelise(chunk):
        lo, up = BOUNDS[chunk], BOUNDS[chunk + 1]
        reads[chunk].wait()

        def one(i, carry):
            f0 = lo + i * BLOCK
            v0 = vbuf[0, pl.ds(f0, BLOCK)].reshape(BLOCK * ANT, CHANNELS)
            v1 = vbuf[1, pl.ds(f0, BLOCK)].reshape(BLOCK * ANT, CHANNELS)
            g = jnp.dot(v0, table[0], preferred_element_type=jnp.float32)
            g = g + jnp.dot(v1, table[1], preferred_element_type=jnp.float32)
            gbuf[pl.ds(pl.multiple_of(f0 * ANT, 8), BLOCK * ANT)] = g
            return carry

        lax.fori_loop(0, (up - lo + BLOCK - 1) // BLOCK, one, 0)

        s0 = chunk * WIDTH * ANT
        size = WIDTH * ANT
        pair = gbuf[pl.ds(s0, size + ANT), 0:128] + gbuf[pl.ds(s0 + 2 * ANT, size + ANT), 128:256]
        total = pair[:size] + pltpu.roll(pair[ANT:], 64, 1)
        cbuf[...] = total
        for a in range(ANT):
            one_ant = cbuf[pl.ds(a, WIDTH, stride=ANT), :]
            turned = one_ant.T[0 : 2 * BAND]
            tbuf[pl.ds(a, 2 * BAND, stride=ANT), :] = turned
        kept = flags[:, pl.ds(chunk * WIDTH, WIDTH)].astype(jnp.float32)
        spectra = tbuf[...].reshape(2, GROUPS, PER, ANT, WIDTH) * kept[None, None, None]
        sbuf[chunk] = spectra.astype(jnp.bfloat16)

    def turn(chunk):
        def send(d, carry):
            j = (k + d) % GROUPS
            pltpu.make_async_remote_copy(
                src_ref=sbuf.at[chunk, :, j],
                dst_ref=rows.at[c, chunk, :, :, k],
                send_sem=turn_send.at[chunk],
                recv_sem=turn_recv.at[chunk],
                device_id=(j, r, c),
                device_id_type=MESH,
            ).start()
            return carry

        lax.fori_loop(1, GROUPS, send, 0)
        pltpu.make_async_copy(sbuf.at[chunk, :, k], rows.at[c, chunk, :, :, k], turn_recv.at[chunk]).start()

    def turned(chunk):
        whole = rows.at[c, chunk]
        pltpu.make_async_copy(whole, whole, turn_recv.at[chunk]).wait()

    def swap(chunk, slot, index):
        copy = pltpu.make_async_remote_copy(
            src_ref=rows.at[slot, chunk],
            dst_ref=rows.at[slot, chunk],
            send_sem=swap_send.at[chunk, index],
            recv_sem=row_recv.at[chunk, slot],
            device_id=mate,
            device_id_type=MESH,
        )
        copy.start()
        return copy

    def line_copy(p, index):
        chunk, source, offset, crosses = PLAN[p][index]
        src = rows.at[c, chunk] if source == p else cols.at[source, chunk]
        dst = rows.at[c, chunk] if crosses else cols.at[source, chunk]
        sem = row_recv.at[chunk, c] if crosses else col_recv.at[chunk, source]
        return pltpu.make_async_remote_copy(
            src_ref=src, dst_ref=dst, send_sem=line_send.at[index], recv_sem=sem,
            device_id=at_plane(offset), device_id_type=MESH,
        )

    def wait_col(chunk, source):
        piece = cols.at[source, chunk]
        pltpu.make_async_copy(piece, piece, col_recv.at[chunk, source]).wait()

    def wait_row(chunk, slot):
        piece = rows.at[slot, chunk]
        pltpu.make_async_copy(piece, piece, row_recv.at[chunk, slot]).wait()

    far = (1 - hi) * 2 + core

    def line(p, chunk):
        got = set()
        for index, (step, source, _, _) in enumerate(PLAN[p]):
            if step != chunk:
                continue
            if source != p and source not in got:
                wait_col(chunk, source)
                got.add(source)
            line_copy(p, index).start()
        for source in range(N_ROW):
            if source != p and source not in got:
                wait_col(chunk, source)

    channelise(0)
    pl.semaphore_wait(barrier, GROUPS - 1 + 5)
    turn(0)
    channelise(1)
    turn(1)
    swaps, owns = [], []
    for chunk in range(CHUNKS):
        turned(chunk)
        for p in range(N_ROW):
            @pl.when(r == p)
            def _(p=p, chunk=chunk):
                line(p, chunk)

        own = pltpu.make_async_copy(rows.at[c, chunk], cols.at[r, chunk], own_sem.at[chunk])
        own.start()
        owns.append(own)
        swaps.append(swap(chunk, c, 0))
        wait_row(chunk, far)
        swaps.append(swap(chunk, far, 1))
    for chunk in range(CHUNKS):
        wait_row(chunk, hi * 2 + other)
        wait_row(chunk, (1 - hi) * 2 + other)
    for copy in owns:
        copy.wait()
    for copy in swaps:
        copy.wait_send()
    for chunk in range(CHUNKS):
        sent = sbuf.at[chunk, :, pl.ds(0, GROUPS - 1)]
        pltpu.make_async_copy(sent, sent, turn_send.at[chunk]).wait()
    for p in range(N_ROW):
        @pl.when(r == p)
        def _(p=p):
            for index in range(len(PLAN[p])):
                line_copy(p, index).wait_send()


def gather(volt, table, flags):
    shape = jax.ShapeDtypeStruct((N_ROW, CHUNKS, 2, PER, GROUPS, ANT, WIDTH), jnp.bfloat16)
    anywhere = pl.BlockSpec(memory_space=pl.ANY)
    inside = pl.BlockSpec(memory_space=pltpu.VMEM)
    most = max(len(plan) for plan in PLAN.values())
    return pl.pallas_call(
        gather_kernel,
        out_shape=(shape, shape),
        in_specs=[anywhere, inside, inside],
        out_specs=(anywhere, anywhere),
        scratch_shapes=[
            pltpu.VMEM((2, PADDED, ANT, CHANNELS), jnp.bfloat16),
            pltpu.VMEM((PADDED * ANT, 256), jnp.float32),
            pltpu.VMEM((WIDTH * ANT, 128), jnp.float32),
            pltpu.VMEM((2 * BAND * ANT, WIDTH), jnp.float32),
            pltpu.VMEM((CHUNKS, 2, GROUPS, PER, ANT, WIDTH), jnp.bfloat16),
            pltpu.SemaphoreType.DMA((CHUNKS,)),
            pltpu.SemaphoreType.DMA((CHUNKS,)),
            pltpu.SemaphoreType.DMA((CHUNKS,)),
            pltpu.SemaphoreType.DMA((CHUNKS,)),
            pltpu.SemaphoreType.DMA((most,)),
            pltpu.SemaphoreType.DMA((CHUNKS, N_ROW)),
            pltpu.SemaphoreType.DMA((CHUNKS, N_ROW)),
            pltpu.SemaphoreType.DMA((CHUNKS, 2)),
        ],
        compiler_params=pltpu.CompilerParams(
            collective_id=0, has_side_effects=True, vmem_limit_bytes=56 * 1024 * 1024
        ),
        name="gather",
    )(volt, table, flags)


def power_kernel(rows, cols, out):
    def laid(ref, q):
        return [ref[:, chunk, q, 0].reshape(N_ROW * GROUPS * ANT, WIDTH) for chunk in range(CHUNKS)]

    re, im = laid(rows, 0), laid(rows, 1)
    first = jnp.concatenate(re + im, axis=1)
    second = jnp.concatenate(im + [-x for x in re], axis=1)
    column = jnp.concatenate(laid(cols, 0) + laid(cols, 1), axis=1)
    for part, left in enumerate((first, second)):
        power = lax.dot_general(left, column, (((1,), (1,)), ((), ())), preferred_element_type=jnp.float32)
        power = power * (1.0 / math.sqrt(SPECTRA))
        for g in range(N_ROW):
            out[part, 0, pl.ds(g, 512, stride=N_ROW), :] = power[:, g * 128 : (g + 1) * 128]


def power(rows, cols):
    spec = pl.BlockSpec((N_ROW, CHUNKS, 2, 1, GROUPS, ANT, WIDTH), lambda j: (0, 0, 0, j, 0, 0, 0))
    return pl.pallas_call(
        power_kernel,
        out_shape=jax.ShapeDtypeStruct((2, PER, 512 * N_ROW, 128), jnp.float32),
        grid=(PER,),
        in_specs=[spec, spec],
        out_specs=pl.BlockSpec((2, 1, 512 * N_ROW, 128), lambda j: (0, j, 0, 0)),
        compiler_params=pltpu.CompilerParams(vmem_limit_bytes=48 * 1024 * 1024),
        name="power",
    )(rows, cols)


def on_device(voltages, fir_window, flags):
    frames = voltages.reshape(2, ANT, FRAMES, CHANNELS).transpose(0, 2, 1, 3)
    weight = (fir_window / math.sqrt(TAPS * CHANNELS)).T
    table = weight[None, :, :, None] * jnp.asarray(basis())[:, :, None, :]
    table = table.astype(jnp.bfloat16).reshape(2, CHANNELS, TAPS * 2 * BAND)
    rows, cols = gather(frames, table, flags)
    return power(rows, cols).reshape(2, PER, 512, N_ROW, 128)


def solution(mesh):
    return jax.shard_map(
        on_device,
        mesh=mesh,
        in_specs=(P(None, ("row", "col", "chan"), None), P(), P(("row", "col", "chan"), None)),
        out_specs=P(None, "chan", "row", None, "col"),
        check_vma=False,
    )
```

time: 221 us -> 66.7 us (0.30)
  waiting for transfers between devices: 133 us -> 0 us
  Pallas kernels: 0 us -> 56.7 us
  matrix products: 27.8 us -> 0 us
  local copies, waits for them, and re-layouts: 25.6 us -> 6.01 us
  blocking collectives: 14.9 us -> 0 us
  between operations: 13.5 us -> 0.04 us
  other arithmetic: 6.14 us -> 3.51 us
    all_gather x1 -> x0, waiting for transfers between devices: 133 us -> none  [on_device(): gathered = lax.all_gather(turned, ('row', 'col'), axis=2, tiled=True)]
    pallas_call x0 -> x2, Pallas kernels: none -> 56.7 us  [the longest x1 53.7 us: gather(): pl.pallas_call(gather_kernel, out_shape=(shape, shape), in_specs=[anywher...]
    dot_general x8 -> x0, matrix products: 27.8 us -> none  [the longest x4 23.3 us: on_device(): jnp.einsum('pasn,pnqk->qkas', filter_frames[:, :, tap:tap + spectra_total...]
    slice x3 -> x0, local copies, waits for them, and re-layouts: 19.8 us -> none  [the longest x1 17.2 us: on_device(): filter_frames[:, :, tap:tap + spectra_total]]
    all_to_all x1 -> x0, blocking collectives: 14.9 us -> none  [on_device(): lax.all_to_all(spectra_rows, 'chan', split_axis=1, concat_axis=2, tiled=T...]
    another operation x2 -> x0, local copies, waits for them, and re-layouts: 4.95 us -> none  [cross_power(): return jnp.stack([real_part, imag_part]) * (1.0 / math.sqrt(spectra_total))]
    mul x1 -> x0, other arithmetic: 4.68 us -> none  [cross_power(): return jnp.stack([real_part, imag_part]) * (1.0 / math.sqrt(spectra_total))]
    mul x0 -> x4, local copies, waits for them, and re-layouts: none -> 3.56 us  [on_device(): table = weight[None, :, :, None] * jnp.asarray(basis())[:, :, None, :]]
  transfers between devices with their start and end apart: 1 -> 0, of which waited for: 1 -> 0; matrix products, arithmetic and copies ran while one was open for 0% -> 0% of each run, Pallas kernels for 0% -> 0%
where the time goes in v1:
time: 66.7 us; the launch traced here: 66.3 us
  Pallas kernels  56.7 us (85%)
  local copies, waits for them, and re-layouts  6.01 us (9%)
  other arithmetic  3.51 us (5%)
    pallas_call x1, Pallas kernels, gather(): pl.pallas_call(gather_kernel, out_shape=(shape, shape), in_specs=[anywher...  53.7 us
    mul x4, local copies, waits for them, and re-layouts, on_device(): table = weight[None, :, :, None] * jnp.asarray(basis())[:, :, None, :]  3.56 us
    pallas_call x1, Pallas kernels, power(): pl.pallas_call(power_kernel, out_shape=jax.ShapeDtypeStruct((2, PER, 512...  2.98 us
    convert_element_type x1, other arithmetic, on_device(): table = table.astype(jnp.bfloat16).reshape(2, CHANNELS, TAPS * 2 * BAND)  2.79 us
    unnamed x4, local copies, waits for them, and re-layouts  2.44 us

profile of v1, /device:TPU:1, one launch (start us, length us, event | category | flops | bytes accessed | tf_op | source)
XLA Modules:
  0.0 66.3 jit_solution(8304357963539108527)
XLA Ops:
  0.0 0.7 %multiply_bitcast_fusion = f32[1024,4]{0,1:T(4,128)S(1)} fusion(f32[4,1024]{1,0:T(4,128)} %param.5), kind=kLoop, calls=%fused_computation.1 | loop fusion | flops 4096 | bytes 32768 | tf_op jit(solution)/shard_map/transpose | solution.py:281
  0.7 0.1 mul.20
  0.8 0.3 copy.6
  1.2 1.3 %mul.23 = f32[2,1024,4,64]{1,3,2,0:T(8,128)S(1)} broadcast(f32[2,1024,64]{1,2,0:T(8,128)} %constant.5.clone), dimensions={0,1,3} | broadcast | bytes 2621440 | tf_op jit(solution)/shard_map/mul | solution.py:282
  2.5 1.8 %copy.7 = f32[2,1024,256]{2,1,0:T(8,128)} copy(f32[2,1024,256]{1,2,0:T(8,128)S(1)} %bitcast.9) | data formatting | bytes 4194304 | tf_op jit(solution)/shard_map/mul | solution.py:282
  4.3 2.8 %multiply_convert_fusion.table = bf16[2,1024,256]{2,1,0:T(8,128)(2,1)} fusion(f32[2,1024,256]{2,1,0:T(8,128)} %copy.7, f32[1024,256]{1,0:T(8,128)S(1)} %copy.6), kind=kLoop, calls=%fused_computation | loop fusion | flops 1048576 | bytes 4194304 | tf_op jit(solution)/shard_map/convert_element_type | solution.py:283
  7.1 53.7 %gather.1 = (bf16[4,2,2,2,16,8,128]{6,5,4,3,2,1,0:T(8,128)(2,1)}, bf16[4,2,2,2,16,8,128]{6,5,4,3,2,1,0:T(8,128)(2,1)}) custom-call(bf16[2,259,8,1024]{3,2,1,0:T(8,128)(2,1)} %bitcast.8, bf16[2,1024,256]{2,1,0:T(8,128)(2,1)} %multiply_convert_fusion.table, s32[8,256]{1,0:T(8,128)} %flags.1), custom_call_target="tpu_custom_call" | custom-call | tf_op jit(solution)/shard_map/gather/pallas_call | solution.py:224
  60.8 0.0 copy-start
  60.8 1.2 %copy-done = bf16[4,2,2,2,16,8,128]{6,5,4,3,2,1,0:T(8,128)(2,1)S(1)} copy-done((bf16[4,2,2,2,16,8,128]{6,5,4,3,2,1,0:T(8,128)(2,1)S(1)}, bf16[4,2,2,2,16,8,128]{6,5,4,3,2,1,0:T(8,128)(2,1)}, u32[]{:S(2)}) %copy-start) | copy-done | bytes 1048600
  62.1 0.0 copy-start.1
  62.1 1.2 %copy-done.1 = bf16[4,2,2,2,16,8,128]{6,5,4,3,2,1,0:T(8,128)(2,1)S(1)} copy-done((bf16[4,2,2,2,16,8,128]{6,5,4,3,2,1,0:T(8,128)(2,1)S(1)}, bf16[4,2,2,2,16,8,128]{6,5,4,3,2,1,0:T(8,128)(2,1)}, u32[]{:S(2)}) %copy-start.1) | copy-done | bytes 1048600
  63.3 3.0 %power.1 = f32[2,2,2048,128]{3,2,1,0:T(8,128)} custom-call(bf16[4,2,2,2,16,8,128]{6,5,4,3,2,1,0:T(8,128)(2,1)S(1)} %copy-done, bf16[4,2,2,2,16,8,128]{6,5,4,3,2,1,0:T(8,128)(2,1)S(1)} %copy-done.1), custom_call_target="tpu_custom_call" | custom-call | tf_op jit(solution)/shard_map/power/pallas_call | solution.py:268
Async XLA Ops:
  60.8 1.2 %copy-start = (bf16[4,2,2,2,16,8,128]{6,5,4,3,2,1,0:T(8,128)(2,1)S(1)}, bf16[4,2,2,2,16,8,128]{6,5,4,3,2,1,0:T(8,128)(2,1)}, u32[]{:S(2)}) copy-start(bf16[4,2,2,2,16,8,128]{6,5,4,3,2,1,0:T(8,128)(2,1)} %get-tuple-element.7.rows) | copy-start | bytes 3145732
  62.1 1.2 %copy-start.1 = (bf16[4,2,2,2,16,8,128]{6,5,4,3,2,1,0:T(8,128)(2,1)S(1)}, bf16[4,2,2,2,16,8,128]{6,5,4,3,2,1,0:T(8,128)(2,1)}, u32[]{:S(2)}) copy-start(bf16[4,2,2,2,16,8,128]{6,5,4,3,2,1,0:T(8,128)(2,1)} %get-tuple-element.8.cols) | copy-start | bytes 3145732

commit v2 on v1

v2 whole, which is shorter than its diff:
```python
import math

import jax
import jax.numpy as jnp
import numpy as np
from jax import lax
from jax.experimental import pallas as pl
from jax.experimental.pallas import tpu as pltpu
from jax.sharding import PartitionSpec as P

MESH = pl.DeviceIdType.MESH

CHANNELS = 1024
TAPS = 4
BAND = 32
SPECTRA = 256
FRAMES = SPECTRA + TAPS - 1
ANT = 8
GROUPS = 16
PER = BAND // GROUPS
N_ROW = 4
PLANES = 8
CHUNKS = 4
WIDTH = SPECTRA // CHUNKS
BOUNDS = (0, 68, 132, 196, FRAMES)
PADDED = 260

PLAN = {
    0: [(0, 1, False), (2, -2, True), (3, -1, True)],
    1: [(1, 1, False), (1, -1, False), (0, 1, False), (2, -1, False), (3, -1, False)],
    2: [(2, -1, False), (2, 1, False), (3, -1, False), (1, 1, False), (0, 1, False)],
    3: [(3, -1, False), (1, 2, True), (0, 1, True)],
}
MOST = 5
LATE = {1: 1, 2: 1}
EARLY = 2
LAG = 2


def steps(p):
    todo = []
    for now in range(CHUNKS + N_ROW - 1):
        step = []
        if now < CHUNKS:
            for index, (source, _, _) in enumerate(PLAN[p]):
                if source == p and (LATE.get(p) != index or now < EARLY):
                    step.append((now, index))
        behind = []
        for index, (source, _, _) in enumerate(PLAN[p]):
            chunk = now - abs(source - p)
            if source != p and 0 <= chunk < CHUNKS:
                behind.append((chunk, index))
        todo.append(step + sorted(behind, key=lambda item: -item[0]))
    if p in LATE:
        todo.append([(chunk, LATE[p]) for chunk in range(EARLY, CHUNKS)])
    return todo[:CHUNKS] + [sum(todo[CHUNKS:], [])]


def basis():
    n = np.arange(CHANNELS)[:, None]
    k = np.arange(BAND)[None, :]
    angle = ((n * k) % CHANNELS).astype(np.float32) * np.float32(2.0 * math.pi / CHANNELS)
    cos, sin = np.cos(angle), np.sin(angle)
    return np.stack([np.concatenate([cos, -sin] * 2, 1), np.concatenate([sin, cos] * 2, 1)])


def gather_kernel(
    volt, waves, window, flags, rows, cols,
    vbuf, wbuf, fbuf, kbuf, table, gbuf, cbuf, tbuf, sbuf,
    volt_sem, small_sem, turn_send, turn_recv, own_sem, line_send, row_recv, col_recv, swap_send,
):
    k = lax.axis_index("chan")
    r = lax.axis_index("row")
    c = lax.axis_index("col")
    hi, core = c // 2, c % 2
    plane = hi * N_ROW + r
    other = 1 - core

    def at_plane(offset):
        z = (plane + offset + PLANES) % PLANES
        return (k, z % N_ROW, (z // N_ROW) * 2 + core)

    mate = (k, r, hi * 2 + other)

    small = [
        pltpu.make_async_copy(window, fbuf, small_sem.at[0]),
        pltpu.make_async_copy(waves, wbuf, small_sem.at[1]),
        pltpu.make_async_copy(flags, kbuf, small_sem.at[2]),
    ]
    reads = []
    for chunk in range(CHUNKS):
        lo, up = BOUNDS[chunk], BOUNDS[chunk + 1]
        reads.append(pltpu.make_async_copy(
            volt.at[:, pl.ds(lo, up - lo)], vbuf.at[:, pl.ds(lo, up - lo)], volt_sem.at[chunk]
        ))
    small[0].start()
    small[1].start()
    reads[0].start()
    small[2].start()
    for copy in reads[1:]:
        copy.start()

    barrier = pltpu.get_barrier_semaphore()

    def greet(d, carry):
        pl.semaphore_signal(barrier, inc=1, device_id=((k + d) % GROUPS, r, c), device_id_type=MESH)
        return carry

    lax.fori_loop(1, GROUPS, greet, 0)
    for offset in (-2, -1, 1, 2):
        pl.semaphore_signal(barrier, inc=1, device_id=at_plane(offset), device_id_type=MESH)
    pl.semaphore_signal(barrier, inc=1, device_id=mate, device_id_type=MESH)

    small[0].wait()
    weight = fbuf[...] * (1.0 / math.sqrt(TAPS * CHANNELS))
    weight = jnp.concatenate([weight, weight], axis=0).T
    small[1].wait()
    lane = lax.broadcasted_iota(jnp.int32, (CHANNELS, 128), 1)
    for half in range(2):
        scale = jnp.where(lane < 64, weight[:, 2 * half : 2 * half + 1], weight[:, 2 * half + 1 : 2 * half + 2])
        for part in range(2):
            table[part, :, half * 128 : (half + 1) * 128] = (wbuf[part] * scale).astype(jnp.bfloat16)

    def channelise(chunk):
        lo, up = BOUNDS[chunk], BOUNDS[chunk + 1]
        reads[chunk].wait()
        block = (min(up + 1, PADDED) - lo) // 2
        for f0 in (lo, lo + block):
            v0 = vbuf[0, f0 : f0 + block].reshape(block * ANT, CHANNELS)
            v1 = vbuf[1, f0 : f0 + block].reshape(block * ANT, CHANNELS)
            g = jnp.dot(v0, table[0], preferred_element_type=jnp.float32)
            g = g + jnp.dot(v1, table[1], preferred_element_type=jnp.float32)
            gbuf[f0 * ANT : (f0 + block) * ANT] = g

        s0 = chunk * WIDTH * ANT
        size = WIDTH * ANT
        pair = gbuf[pl.ds(s0, size + ANT), 0:128] + gbuf[pl.ds(s0 + 2 * ANT, size + ANT), 128:256]
        cbuf[...] = pair[:size] + pltpu.roll(pair[ANT:], 64, 1)
        for a in range(ANT):
            turned = cbuf[pl.ds(a, WIDTH, stride=ANT), :].T
            both = jnp.concatenate([turned[0:BAND], turned[BAND : 2 * BAND]], axis=1)
            tbuf[pl.ds(a, BAND, stride=ANT), :] = both
        if chunk == 0:
            small[2].wait()
        kept = kbuf[:, chunk * WIDTH : (chunk + 1) * WIDTH].astype(jnp.float32)
        kept = jnp.concatenate([kept, kept], axis=1)
        spectra = tbuf[...].reshape(GROUPS, PER, ANT, 2 * WIDTH) * kept[None, None]
        sbuf[chunk] = spectra.astype(jnp.bfloat16)

    def turn(chunk):
        def send(d, carry):
            j = (k + d) % GROUPS
            pltpu.make_async_remote_copy(
                src_ref=sbuf.at[chunk, j],
                dst_ref=rows.at[c, chunk, :, k],
                send_sem=turn_send.at[chunk],
                recv_sem=turn_recv.at[chunk],
                device_id=(j, r, c),
                device_id_type=MESH,
            ).start()
            return carry

        lax.fori_loop(1, GROUPS, send, 0)
        pltpu.make_async_copy(sbuf.at[chunk, k], rows.at[c, chunk, :, k], turn_recv.at[chunk]).start()

    def turned(chunk):
        whole = rows.at[c, chunk]
        pltpu.make_async_copy(whole, whole, turn_recv.at[chunk]).wait()

    def swap(chunk, slot, index):
        copy = pltpu.make_async_remote_copy(
            src_ref=rows.at[slot, chunk],
            dst_ref=rows.at[slot, chunk],
            send_sem=swap_send.at[chunk, index],
            recv_sem=row_recv.at[chunk, slot],
            device_id=mate,
            device_id_type=MESH,
        )
        copy.start()
        return copy

    def line_copy(p, chunk, index):
        source, offset, crosses = PLAN[p][index]
        src = rows.at[c, chunk] if source == p else cols.at[source, chunk]
        dst = rows.at[c, chunk] if crosses else cols.at[source, chunk]
        sem = row_recv.at[chunk, c] if crosses else col_recv.at[chunk, source]
        return pltpu.make_async_remote_copy(
            src_ref=src, dst_ref=dst, send_sem=line_send.at[chunk, index], recv_sem=sem,
            device_id=at_plane(offset), device_id_type=MESH,
        )

    def wait_col(chunk, source):
        piece = cols.at[source, chunk]
        pltpu.make_async_copy(piece, piece, col_recv.at[chunk, source]).wait()

    def wait_row(chunk, slot):
        piece = rows.at[slot, chunk]
        pltpu.make_async_copy(piece, piece, row_recv.at[chunk, slot]).wait()

    far = (1 - hi) * 2 + core

    def each_place(act):
        for p in range(N_ROW):
            @pl.when(r == p)
            def _(p=p):
                act(p)

    def send_step(p, step):
        for chunk, index in steps(p)[step]:
            source = PLAN[p][index][0]
            if source != p:
                wait_col(chunk, source)
            line_copy(p, chunk, index).start()
        if step == CHUNKS:
            relayed = [source for source, _, _ in PLAN[p]]
            for source in range(N_ROW):
                if source not in relayed:
                    for chunk in range(CHUNKS):
                        wait_col(chunk, source)

    swaps, owns = [], []

    def sends(chunk):
        turned(chunk)
        each_place(lambda p: send_step(p, chunk))
        own = pltpu.make_async_copy(rows.at[c, chunk], cols.at[r, chunk], own_sem.at[chunk])
        own.start()
        owns.append(own)
        swaps.append(swap(chunk, c, 0))

    for chunk in range(CHUNKS):
        channelise(chunk)
        if chunk == 0:
            pl.semaphore_wait(barrier, GROUPS - 1 + 5)
        turn(chunk)
        if chunk >= LAG:
            sends(chunk - LAG)
    for chunk in range(CHUNKS - LAG, CHUNKS):
        sends(chunk)
    each_place(lambda p: send_step(p, CHUNKS))
    for chunk in range(CHUNKS):
        wait_row(chunk, far)
        swaps.append(swap(chunk, far, 1))
    for copy in owns:
        copy.wait()
    for chunk in range(CHUNKS):
        sent = sbuf.at[chunk, pl.ds(0, GROUPS - 1)]
        pltpu.make_async_copy(sent, sent, turn_send.at[chunk]).wait()
    for copy in swaps:
        copy.wait_send()

    def finish(p):
        for chunk in range(CHUNKS):
            for index in range(len(PLAN[p])):
                line_copy(p, chunk, index).wait_send()

    each_place(finish)
    for chunk in range(CHUNKS):
        wait_row(chunk, hi * 2 + other)
        wait_row(chunk, (1 - hi) * 2 + other)


def gather(volt, window, flags):
    shape = jax.ShapeDtypeStruct((N_ROW, CHUNKS, PER, GROUPS, ANT, 2 * WIDTH), jnp.bfloat16)
    anywhere = pl.BlockSpec(memory_space=pltpu.HBM)
    inside = pl.BlockSpec(memory_space=pltpu.VMEM)
    return pl.pallas_call(
        gather_kernel,
        out_shape=(shape, shape),
        in_specs=[anywhere] * 4,
        out_specs=(inside, inside),
        scratch_shapes=[
            pltpu.VMEM((2, PADDED, ANT, CHANNELS), jnp.bfloat16),
            pltpu.VMEM((2, CHANNELS, 128), jnp.float32),
            pltpu.VMEM((TAPS, CHANNELS), jnp.float32),
            pltpu.VMEM((ANT, SPECTRA), jnp.int32),
            pltpu.VMEM((2, CHANNELS, 256), jnp.bfloat16),
            pltpu.VMEM((PADDED * ANT, 256), jnp.float32),
            pltpu.VMEM((WIDTH * ANT, 128), jnp.float32),
            pltpu.VMEM((BAND * ANT, 2 * WIDTH), jnp.float32),
            pltpu.VMEM((CHUNKS, GROUPS, PER, ANT, 2 * WIDTH), jnp.bfloat16),
            pltpu.SemaphoreType.DMA((CHUNKS,)),
            pltpu.SemaphoreType.DMA((3,)),
            pltpu.SemaphoreType.DMA((CHUNKS,)),
            pltpu.SemaphoreType.DMA((CHUNKS,)),
            pltpu.SemaphoreType.DMA((CHUNKS,)),
            pltpu.SemaphoreType.DMA((CHUNKS, MOST)),
            pltpu.SemaphoreType.DMA((CHUNKS, N_ROW)),
            pltpu.SemaphoreType.DMA((CHUNKS, N_ROW)),
            pltpu.SemaphoreType.DMA((CHUNKS, 2)),
        ],
        compiler_params=pltpu.CompilerParams(
            collective_id=0, has_side_effects=True, vmem_limit_bytes=40 * 1024 * 1024
        ),
        name="gather",
    )(*(pltpu.with_memory_space_constraint(x, pltpu.HBM) for x in (volt, jnp.asarray(basis()), window, flags)))


def power_kernel(rows, cols, out):
    ch = pl.program_id(0)
    half = pl.program_id(1)
    side = N_ROW // 2
    here = [rows[pl.ds(half * side, side), t, ch].reshape(side * GROUPS * ANT, 2 * WIDTH) for t in range(CHUNKS)]
    turned = [jnp.concatenate([x[:, WIDTH:], -x[:, :WIDTH]], axis=1) for x in here]
    first = jnp.concatenate(here, axis=1)
    second = jnp.concatenate(turned, axis=1)
    column = jnp.concatenate(
        [cols[:, t, ch].reshape(N_ROW * GROUPS * ANT, 2 * WIDTH) for t in range(CHUNKS)], axis=1
    )
    for part, left in enumerate((first, second)):
        power = lax.dot_general(left, column, (((1,), (1,)), ((), ())), preferred_element_type=jnp.float32)
        power = power * (1.0 / math.sqrt(SPECTRA))
        for g in range(N_ROW):
            out[part, 0, pl.ds(g, side * 128, stride=N_ROW), :] = power[:, g * 128 : (g + 1) * 128]


def power(rows, cols):
    inside = pl.BlockSpec(memory_space=pltpu.VMEM)
    return pl.pallas_call(
        power_kernel,
        out_shape=jax.ShapeDtypeStruct((2, PER, 512 * N_ROW, 128), jnp.float32),
        grid=(PER, 2),
        in_specs=[inside, inside],
        out_specs=pl.BlockSpec((2, 1, 256 * N_ROW, 128), lambda j, half: (0, j, half, 0)),
        compiler_params=pltpu.CompilerParams(vmem_limit_bytes=48 * 1024 * 1024),
        name="power",
    )(rows, cols)


def on_device(voltages, fir_window, flags):
    frames = voltages.reshape(2, ANT, FRAMES, CHANNELS).transpose(0, 2, 1, 3)
    rows, cols = gather(frames, fir_window, flags)
    return power(rows, cols).reshape(2, PER, 512, N_ROW, 128)


def solution(mesh):
    return jax.shard_map(
        on_device,
        mesh=mesh,
        in_specs=(P(None, ("row", "col", "chan"), None), P(), P(("row", "col", "chan"), None)),
        out_specs=P(None, "chan", "row", None, "col"),
        check_vma=False,
    )
```

time: 66.7 us -> 45.3 us (0.68)
  Pallas kernels: 56.7 us -> 45.3 us
  local copies, waits for them, and re-layouts: 6.01 us -> 0 us
  other arithmetic: 3.51 us -> 0 us
    pallas_call x1, Pallas kernels: 53.7 us -> 41.8 us  [gather(): pl.pallas_call(gather_kernel, out_shape=(shape, shape), in_specs=[anywher...]
    mul x4 -> x0, local copies, waits for them, and re-layouts: 3.56 us -> none  [on_device(): table = weight[None, :, :, None] * jnp.asarray(basis())[:, :, None, :]]
    convert_element_type x1 -> x0, other arithmetic: 2.79 us -> none  [on_device(): table = table.astype(jnp.bfloat16).reshape(2, CHANNELS, TAPS * 2 * BAND)]
    unnamed x4 -> x0, local copies, waits for them, and re-layouts: 2.44 us -> none
    transpose x1 -> x0, other arithmetic: 0.72 us -> none  [on_device(): weight = (fir_window / math.sqrt(TAPS * CHANNELS)).T]
where the time goes in v2:
time: 45.3 us
  Pallas kernels  45.3 us (100%)
    pallas_call x1, Pallas kernels, gather(): pl.pallas_call(gather_kernel, out_shape=(shape, shape), in_specs=[anywher...  41.8 us
    pallas_call x1, Pallas kernels, power(): pl.pallas_call(power_kernel, out_shape=jax.ShapeDtypeStruct((2, PER, 512...  3.42 us

profile of v2, /device:TPU:1, one launch (start us, length us, event | category | flops | bytes accessed | tf_op | source)
XLA Modules:
  0.0 45.3 jit_solution(16090388608538045446)
XLA Ops:
  0.0 41.8 %gather.1 = (bf16[4,4,2,16,8,128]{5,4,3,2,1,0:T(8,128)(2,1)S(1)}, bf16[4,4,2,16,8,128]{5,4,3,2,1,0:T(8,128)(2,1)S(1)}) custom-call(bf16[2,259,8,1024]{3,2,1,0:T(8,128)(2,1)} %bitcast.4, f32[2,1024,128]{2,1,0:T(8,128)} %constant.2.clone.waves, f32[4,1024]{1,0:T(4,128)} %window.1, s32[8,256]{1,0:T(8,128)} %flags.1), custom_call_target="tpu_custom_call" | custom-call | tf_op jit(solution)/shard_map/gather/pallas_call | solution.py:267
  41.8 3.4 %power.1 = f32[2,2,2048,128]{3,2,1,0:T(8,128)} custom-call(bf16[4,4,2,16,8,128]{5,4,3,2,1,0:T(8,128)(2,1)S(1)} %get-tuple-element.7.rows, bf16[4,4,2,16,8,128]{5,4,3,2,1,0:T(8,128)(2,1)S(1)} %get-tuple-element.8.cols), custom_call_target="tpu_custom_call" | custom-call | tf_op jit(solution)/shard_map/power/pallas_call | solution.py:319

commit v3 on v2

--- a/solution.py
+++ b/solution.py
@@ -25,35 +25,29 @@
 BOUNDS = (0, 68, 132, 196, FRAMES)
 PADDED = 260
 
-PLAN = {
-    0: [(0, 1, False), (2, -2, True), (3, -1, True)],
-    1: [(1, 1, False), (1, -1, False), (0, 1, False), (2, -1, False), (3, -1, False)],
-    2: [(2, -1, False), (2, 1, False), (3, -1, False), (1, 1, False), (0, 1, False)],
-    3: [(3, -1, False), (1, 2, True), (0, 1, True)],
+ORDER = {
+    0: [
+        (0, 0, 1), (0, 1, 1), (0, 2, 1), (0, 3, 1), (2, 0, -2), (2, 1, -2), (2, 2, -2), (3, 0, -1),
+        (3, 1, -1), (3, 2, -1), (3, 3, -1), (2, 3, -2),
+    ],
+    1: [
+        (1, 0, -1), (1, 0, 1), (1, 1, -1), (1, 1, 1), (1, 2, -1), (1, 2, 1), (0, 0, 1), (2, 0, -1),
+        (0, 1, 1), (2, 1, -1), (0, 2, 1), (2, 2, -1), (0, 3, 1), (3, 0, -1), (1, 3, 1), (3, 1, -1),
+        (3, 2, -1), (3, 3, -1), (2, 3, -1), (1, 3, -1),
+    ],
+    2: [
+        (2, 0, -1), (2, 0, 1), (2, 1, -1), (2, 1, 1), (2, 2, -1), (2, 2, 1), (1, 0, 1), (3, 0, -1),
+        (1, 1, 1), (3, 1, -1), (1, 2, 1), (3, 2, -1), (0, 0, 1), (3, 3, -1), (0, 1, 1), (2, 3, -1),
+        (0, 2, 1), (0, 3, 1), (1, 3, 1), (2, 3, 1),
+    ],
+    3: [
+        (3, 0, -1), (3, 1, -1), (3, 2, -1), (3, 3, -1), (1, 0, 2), (1, 1, 2), (1, 2, 2), (0, 0, 1),
+        (0, 1, 1), (0, 2, 1), (0, 3, 1), (1, 3, 2),
+    ],
 }
-MOST = 5
-LATE = {1: 1, 2: 1}
-EARLY = 2
-LAG = 2
-
-
-def steps(p):
-    todo = []
-    for now in range(CHUNKS + N_ROW - 1):
-        step = []
-        if now < CHUNKS:
-            for index, (source, _, _) in enumerate(PLAN[p]):
-                if source == p and (LATE.get(p) != index or now < EARLY):
-                    step.append((now, index))
-        behind = []
-        for index, (source, _, _) in enumerate(PLAN[p]):
-            chunk = now - abs(source - p)
-            if source != p and 0 <= chunk < CHUNKS:
-                behind.append((chunk, index))
-        todo.append(step + sorted(behind, key=lambda item: -item[0]))
-    if p in LATE:
-        todo.append([(chunk, LATE[p]) for chunk in range(EARLY, CHUNKS)])
-    return todo[:CHUNKS] + [sum(todo[CHUNKS:], [])]
+MOST = 20
+PIECES = 4
+LAG = 3
 
 
 def basis():
@@ -97,8 +91,6 @@
     small[1].start()
     reads[0].start()
     small[2].start()
-    for copy in reads[1:]:
-        copy.start()
 
     barrier = pltpu.get_barrier_semaphore()
 
@@ -124,6 +116,9 @@
     def channelise(chunk):
         lo, up = BOUNDS[chunk], BOUNDS[chunk + 1]
         reads[chunk].wait()
+        if chunk == 0:
+            for copy in reads[1:]:
+                copy.start()
         block = (min(up + 1, PADDED) - lo) // 2
         for f0 in (lo, lo + block):
             v0 = vbuf[0, f0 : f0 + block].reshape(block * ANT, CHANNELS)
@@ -179,13 +174,14 @@
         copy.start()
         return copy
 
-    def line_copy(p, chunk, index):
-        source, offset, crosses = PLAN[p][index]
+    def line_copy(p, index):
+        source, chunk, offset = ORDER[p][index]
+        crosses = not 0 <= p + offset < N_ROW
         src = rows.at[c, chunk] if source == p else cols.at[source, chunk]
         dst = rows.at[c, chunk] if crosses else cols.at[source, chunk]
         sem = row_recv.at[chunk, c] if crosses else col_recv.at[chunk, source]
         return pltpu.make_async_remote_copy(
-            src_ref=src, dst_ref=dst, send_sem=line_send.at[chunk, index], recv_sem=sem,
+            src_ref=src, dst_ref=dst, send_sem=line_send.at[index], recv_sem=sem,
             device_id=at_plane(offset), device_id_type=MESH,
         )
 
@@ -205,28 +201,34 @@
             def _(p=p):
                 act(p)
 
-    def send_step(p, step):
-        for chunk, index in steps(p)[step]:
-            source = PLAN[p][index][0]
-            if source != p:
-                wait_col(chunk, source)
-            line_copy(p, chunk, index).start()
-        if step == CHUNKS:
-            relayed = [source for source, _, _ in PLAN[p]]
+    def first_need(p, chunk):
+        for index, (source, step, _) in enumerate(ORDER[p]):
+            if (source == p and step >= chunk) or (source != p and chunk < CHUNKS):
+                return index
+        return len(ORDER[p])
+
+    def send_step(p, chunk):
+        for index in range(first_need(p, chunk), first_need(p, chunk + 1)):
+            source, step, _ = ORDER[p][index]
+            if source != p and all(item[:2] != (source, step) for item in ORDER[p][:index]):
+                wait_col(step, source)
+            line_copy(p, index).start()
+        if chunk == CHUNKS - 1:
+            relayed = [item[:2] for item in ORDER[p]]
             for source in range(N_ROW):
-                if source not in relayed:
-                    for chunk in range(CHUNKS):
-                        wait_col(chunk, source)
+                for step in range(CHUNKS):
+                    if source != p and (source, step) not in relayed:
+                        wait_col(step, source)
 
     swaps, owns = [], []
 
     def sends(chunk):
         turned(chunk)
-        each_place(lambda p: send_step(p, chunk))
+        swaps.append(swap(chunk, c, 0))
         own = pltpu.make_async_copy(rows.at[c, chunk], cols.at[r, chunk], own_sem.at[chunk])
         own.start()
         owns.append(own)
-        swaps.append(swap(chunk, c, 0))
+        each_place(lambda p: send_step(p, chunk))
 
     for chunk in range(CHUNKS):
         channelise(chunk)
@@ -237,7 +239,6 @@
             sends(chunk - LAG)
     for chunk in range(CHUNKS - LAG, CHUNKS):
         sends(chunk)
-    each_place(lambda p: send_step(p, CHUNKS))
     for chunk in range(CHUNKS):
         wait_row(chunk, far)
         swaps.append(swap(chunk, far, 1))
@@ -250,9 +251,8 @@
         copy.wait_send()
 
     def finish(p):
-        for chunk in range(CHUNKS):
-            for index in range(len(PLAN[p])):
-                line_copy(p, chunk, index).wait_send()
+        for index in range(len(ORDER[p])):
+            line_copy(p, index).wait_send()
 
     each_place(finish)
     for chunk in range(CHUNKS):
@@ -284,7 +284,7 @@
             pltpu.SemaphoreType.DMA((CHUNKS,)),
             pltpu.SemaphoreType.DMA((CHUNKS,)),
             pltpu.SemaphoreType.DMA((CHUNKS,)),
-            pltpu.SemaphoreType.DMA((CHUNKS, MOST)),
+            pltpu.SemaphoreType.DMA((MOST,)),
             pltpu.SemaphoreType.DMA((CHUNKS, N_ROW)),
             pltpu.SemaphoreType.DMA((CHUNKS, N_ROW)),
             pltpu.SemaphoreType.DMA((CHUNKS, 2)),
@@ -296,22 +296,30 @@
     )(*(pltpu.with_memory_space_constraint(x, pltpu.HBM) for x in (volt, jnp.asarray(basis()), window, flags)))
 
 
-def power_kernel(rows, cols, out):
-    ch = pl.program_id(0)
-    half = pl.program_id(1)
-    side = N_ROW // 2
-    here = [rows[pl.ds(half * side, side), t, ch].reshape(side * GROUPS * ANT, 2 * WIDTH) for t in range(CHUNKS)]
-    turned = [jnp.concatenate([x[:, WIDTH:], -x[:, :WIDTH]], axis=1) for x in here]
-    first = jnp.concatenate(here, axis=1)
-    second = jnp.concatenate(turned, axis=1)
-    column = jnp.concatenate(
-        [cols[:, t, ch].reshape(N_ROW * GROUPS * ANT, 2 * WIDTH) for t in range(CHUNKS)], axis=1
-    )
-    for part, left in enumerate((first, second)):
-        power = lax.dot_general(left, column, (((1,), (1,)), ((), ())), preferred_element_type=jnp.float32)
-        power = power * (1.0 / math.sqrt(SPECTRA))
-        for g in range(N_ROW):
-            out[part, 0, pl.ds(g, side * 128, stride=N_ROW), :] = power[:, g * 128 : (g + 1) * 128]
+def power_kernel(rows, cols, out, held, sem):
+    side = 512 // PIECES
+    copies = []
+    for ch in range(PER):
+        row, col = (
+            [ref[:, t, ch].reshape(N_ROW * GROUPS * ANT, 2 * WIDTH) for t in range(CHUNKS)] for ref in (rows, cols)
+        )
+        column = jnp.concatenate(col, axis=1)
+        for piece in range(PIECES):
+            here = [x[piece * side : (piece + 1) * side] for x in row]
+            turned = [jnp.concatenate([x[:, WIDTH:], -x[:, :WIDTH]], axis=1) for x in here]
+            left = jnp.concatenate([jnp.concatenate(here, axis=1), jnp.concatenate(turned, axis=1)], axis=0)
+            power = lax.dot_general(left, column, (((1,), (1,)), ((), ())), preferred_element_type=jnp.float32)
+            power = power * (1.0 / math.sqrt(SPECTRA))
+            for part in range(2):
+                for g in range(N_ROW):
+                    block = power[part * side : (part + 1) * side, g * 128 : (g + 1) * 128]
+                    held[ch, piece, part, pl.ds(g, side, stride=N_ROW), :] = block
+            lines = pl.ds(piece * side * N_ROW, side * N_ROW)
+            copy = pltpu.make_async_copy(held.at[ch, piece], out.at[:, ch, lines], sem.at[ch, piece])
+            copy.start()
+            copies.append(copy)
+    for copy in copies:
+        copy.wait()
 
 
 def power(rows, cols):
@@ -319,10 +327,13 @@
     return pl.pallas_call(
         power_kernel,
         out_shape=jax.ShapeDtypeStruct((2, PER, 512 * N_ROW, 128), jnp.float32),
-        grid=(PER, 2),
         in_specs=[inside, inside],
-        out_specs=pl.BlockSpec((2, 1, 256 * N_ROW, 128), lambda j, half: (0, j, half, 0)),
-        compiler_params=pltpu.CompilerParams(vmem_limit_bytes=48 * 1024 * 1024),
+        out_specs=pl.BlockSpec(memory_space=pltpu.HBM),
+        scratch_shapes=[
+            pltpu.VMEM((PER, PIECES, 2, 512 * N_ROW // PIECES, 128), jnp.float32),
+            pltpu.SemaphoreType.DMA((PER, PIECES)),
+        ],
+        compiler_params=pltpu.CompilerParams(vmem_limit_bytes=40 * 1024 * 1024),
         name="power",
     )(rows, cols)
 

time: 45.3 us -> 40.9 us (0.903)
  Pallas kernels: 45.3 us -> 40.7 us
    pallas_call x1, Pallas kernels: 41.8 us -> 38.3 us  [gather(): pl.pallas_call(gather_kernel, out_shape=(shape, shape), in_specs=[anywher...]
    pallas_call x1, Pallas kernels: 3.42 us -> 2.41 us  [power(): pl.pallas_call(power_kernel, out_shape=jax.ShapeDtypeStruct((2, PER, 512...]
where the time goes in v3:
time: 40.9 us; the launch traced here: 40.7 us
  Pallas kernels  40.7 us (100%)
    pallas_call x1, Pallas kernels, gather(): pl.pallas_call(gather_kernel, out_shape=(shape, shape), in_specs=[anywher...  38.3 us
    pallas_call x1, Pallas kernels, power(): pl.pallas_call(power_kernel, out_shape=jax.ShapeDtypeStruct((2, PER, 512...  2.41 us

profile of v3, /device:TPU:1, one launch (start us, length us, event | category | flops | bytes accessed | tf_op | source)
XLA Modules:
  0.0 40.7 jit_solution(18307440629439279688)
XLA Ops:
  0.0 38.3 %gather.1 = (bf16[4,4,2,16,8,128]{5,4,3,2,1,0:T(8,128)(2,1)S(1)}, bf16[4,4,2,16,8,128]{5,4,3,2,1,0:T(8,128)(2,1)S(1)}) custom-call(bf16[2,259,8,1024]{3,2,1,0:T(8,128)(2,1)} %bitcast.4, f32[2,1024,128]{2,1,0:T(8,128)} %constant.2.clone.waves, f32[4,1024]{1,0:T(4,128)} %window.1, s32[8,256]{1,0:T(8,128)} %flags.1), custom_call_target="tpu_custom_call" | custom-call | tf_op jit(solution)/shard_map/gather/pallas_call | solution.py:267
  38.3 2.4 %power.1 = f32[2,2,2048,128]{3,2,1,0:T(8,128)} custom-call(bf16[4,4,2,16,8,128]{5,4,3,2,1,0:T(8,128)(2,1)S(1)} %get-tuple-element.7.rows, bf16[4,4,2,16,8,128]{5,4,3,2,1,0:T(8,128)(2,1)S(1)} %get-tuple-element.8.cols), custom_call_target="tpu_custom_call" | custom-call | tf_op jit(solution)/shard_map/power/pallas_call | solution.py:327

commit v4 on v3

--- a/solution.py
+++ b/solution.py
@@ -27,25 +27,45 @@
 
 ORDER = {
     0: [
-        (0, 0, 1), (0, 1, 1), (0, 2, 1), (0, 3, 1), (2, 0, -2), (2, 1, -2), (2, 2, -2), (3, 0, -1),
-        (3, 1, -1), (3, 2, -1), (3, 3, -1), (2, 3, -2),
+        (0, 0, 1), (0, 1, 1), (0, 2, 1), (0, 3, 1), (2, 0, 6), (2, 1, 6), (2, 2, 6), (3, 0, 7),
+        (3, 1, 7), (3, 2, 7), (2, 3, 6), (3, 3, 7),
     ],
     1: [
-        (1, 0, -1), (1, 0, 1), (1, 1, -1), (1, 1, 1), (1, 2, -1), (1, 2, 1), (0, 0, 1), (2, 0, -1),
-        (0, 1, 1), (2, 1, -1), (0, 2, 1), (2, 2, -1), (0, 3, 1), (3, 0, -1), (1, 3, 1), (3, 1, -1),
-        (3, 2, -1), (3, 3, -1), (2, 3, -1), (1, 3, -1),
+        (1, 0, 0), (1, 0, 2), (1, 1, 0), (1, 1, 2), (1, 2, 0), (1, 2, 2), (0, 0, 2), (2, 0, 0),
+        (0, 1, 2), (2, 1, 0), (0, 2, 2), (2, 2, 0), (1, 3, 2), (3, 0, 0), (0, 3, 2), (3, 1, 0),
+        (3, 2, 0), (2, 3, 0), (3, 3, 0), (4, 3, 0), (1, 3, 0),
     ],
     2: [
-        (2, 0, -1), (2, 0, 1), (2, 1, -1), (2, 1, 1), (2, 2, -1), (2, 2, 1), (1, 0, 1), (3, 0, -1),
-        (1, 1, 1), (3, 1, -1), (1, 2, 1), (3, 2, -1), (0, 0, 1), (3, 3, -1), (0, 1, 1), (2, 3, -1),
-        (0, 2, 1), (0, 3, 1), (1, 3, 1), (2, 3, 1),
+        (2, 0, 1), (2, 0, 3), (2, 1, 1), (2, 1, 3), (2, 2, 1), (2, 2, 3), (1, 0, 3), (3, 0, 1),
+        (1, 1, 3), (3, 1, 1), (1, 2, 3), (3, 2, 1), (0, 0, 3), (2, 3, 1), (0, 1, 3), (3, 3, 1),
+        (0, 2, 3), (1, 3, 3), (0, 3, 3), (7, 3, 3), (2, 3, 3),
     ],
     3: [
-        (3, 0, -1), (3, 1, -1), (3, 2, -1), (3, 3, -1), (1, 0, 2), (1, 1, 2), (1, 2, 2), (0, 0, 1),
-        (0, 1, 1), (0, 2, 1), (0, 3, 1), (1, 3, 2),
+        (3, 0, 2), (3, 1, 2), (3, 2, 2), (3, 3, 2), (1, 0, 5), (1, 1, 5), (1, 2, 5), (0, 0, 4),
+        (0, 1, 4), (0, 2, 4), (1, 3, 5), (0, 3, 4),
+    ],
+    4: [
+        (4, 0, 5), (4, 1, 5), (4, 2, 5), (4, 3, 1), (4, 3, 5), (6, 0, 2), (6, 1, 2), (6, 2, 2),
+        (7, 0, 3), (7, 1, 3), (7, 2, 3), (6, 3, 2),
+    ],
+    5: [
+        (5, 0, 4), (5, 0, 6), (5, 1, 4), (5, 1, 6), (5, 2, 4), (5, 2, 6), (4, 0, 6), (6, 0, 4),
+        (4, 1, 6), (6, 1, 4), (4, 2, 6), (6, 2, 4), (5, 3, 6), (7, 0, 4), (4, 3, 6), (7, 1, 4),
+        (7, 2, 4), (6, 3, 4), (5, 3, 4), (7, 3, 4),
+    ],
+    6: [
+        (6, 0, 5), (6, 0, 7), (6, 1, 5), (6, 1, 7), (6, 2, 5), (6, 2, 7), (5, 0, 7), (7, 0, 5),
+        (5, 1, 7), (7, 1, 5), (5, 2, 7), (7, 2, 5), (4, 0, 7), (6, 3, 5), (4, 1, 7), (7, 3, 5),
+        (4, 2, 7), (5, 3, 7), (6, 3, 7), (4, 3, 7),
+    ],
+    7: [
+        (7, 0, 6), (7, 1, 6), (7, 2, 6), (7, 3, 2), (7, 3, 6), (5, 0, 1), (5, 1, 1), (5, 2, 1),
+        (4, 0, 0), (4, 1, 0), (4, 2, 0), (5, 3, 1),
     ],
 }
-MOST = 20
+HOPS = (3,)
+CROSSING = sorted({(z, t) for z, sends in ORDER.items() for _, _, t in sends if z // N_ROW != t // N_ROW})
+MOST = 21
 PIECES = 4
 LAG = 3
 
@@ -60,8 +80,8 @@
 
 def gather_kernel(
     volt, waves, window, flags, rows, cols,
-    vbuf, wbuf, fbuf, kbuf, table, gbuf, cbuf, tbuf, sbuf,
-    volt_sem, small_sem, turn_send, turn_recv, own_sem, line_send, row_recv, col_recv, swap_send,
+    vbuf, wbuf, fbuf, kbuf, table, gbuf, cbuf, tbuf, sbuf, hop,
+    volt_sem, small_sem, turn_send, turn_recv, own_sem, line_send, row_recv, col_recv, swap_send, hop_recv, answer,
 ):
     k = lax.axis_index("chan")
     r = lax.axis_index("row")
@@ -70,8 +90,7 @@
     plane = hi * N_ROW + r
     other = 1 - core
 
-    def at_plane(offset):
-        z = (plane + offset + PLANES) % PLANES
+    def at_plane(z):
         return (k, z % N_ROW, (z // N_ROW) * 2 + core)
 
     mate = (k, r, hi * 2 + other)
@@ -99,8 +118,8 @@
         return carry
 
     lax.fori_loop(1, GROUPS, greet, 0)
-    for offset in (-2, -1, 1, 2):
-        pl.semaphore_signal(barrier, inc=1, device_id=at_plane(offset), device_id_type=MESH)
+    for offset in range(1, N_ROW):
+        pl.semaphore_signal(barrier, inc=1, device_id=(k, (r + offset) % N_ROW, c), device_id_type=MESH)
     pl.semaphore_signal(barrier, inc=1, device_id=mate, device_id_type=MESH)
 
     small[0].wait()
@@ -174,16 +193,30 @@
         copy.start()
         return copy
 
-    def line_copy(p, index):
-        source, chunk, offset = ORDER[p][index]
-        crosses = not 0 <= p + offset < N_ROW
-        src = rows.at[c, chunk] if source == p else cols.at[source, chunk]
-        dst = rows.at[c, chunk] if crosses else cols.at[source, chunk]
-        sem = row_recv.at[chunk, c] if crosses else col_recv.at[chunk, source]
+    def line_copy(z, index):
+        source, chunk, target = ORDER[z][index]
+        line, place = source // N_ROW, source % N_ROW
+        slot = line * 2 + core
+        if source == z:
+            src = rows.at[slot, chunk]
+        elif line == z // N_ROW:
+            src = cols.at[place, chunk]
+        else:
+            src = hop.at[HOPS.index(chunk)]
+        if line == target // N_ROW:
+            dst, sem = cols.at[place, chunk], col_recv.at[chunk, place]
+        elif target == (source + N_ROW) % PLANES:
+            dst, sem = rows.at[slot, chunk], row_recv.at[chunk, slot]
+        else:
+            dst, sem = hop.at[HOPS.index(chunk)], hop_recv.at[HOPS.index(chunk)]
         return pltpu.make_async_remote_copy(
             src_ref=src, dst_ref=dst, send_sem=line_send.at[index], recv_sem=sem,
-            device_id=at_plane(offset), device_id_type=MESH,
+            device_id=at_plane(target), device_id_type=MESH,
         )
+
+    def wait_hop(chunk):
+        piece = hop.at[HOPS.index(chunk)]
+        pltpu.make_async_copy(piece, piece, hop_recv.at[HOPS.index(chunk)]).wait()
 
     def wait_col(chunk, source):
         piece = cols.at[source, chunk]
@@ -195,30 +228,49 @@
 
     far = (1 - hi) * 2 + core
 
-    def each_place(act):
-        for p in range(N_ROW):
-            @pl.when(r == p)
-            def _(p=p):
-                act(p)
-
-    def first_need(p, chunk):
-        for index, (source, step, _) in enumerate(ORDER[p]):
-            if (source == p and step >= chunk) or (source != p and chunk < CHUNKS):
+    def each_plane(act):
+        for z in range(PLANES):
+            @pl.when(plane == z)
+            def _(z=z):
+                act(z)
+
+    def enter(z):
+        near = GROUPS - 1 + N_ROW - 1 + 1
+        partners = sorted({pair[0] + pair[1] - z for pair in CROSSING if z in pair})
+        if z < N_ROW:
+            pl.semaphore_wait(barrier, near)
+            for partner in partners:
+                pl.semaphore_signal(barrier, inc=1, device_id=at_plane(partner), device_id_type=MESH)
+        else:
+            pl.semaphore_wait(barrier, near + len(partners))
+            for sender, target in CROSSING:
+                if target == z:
+                    pl.semaphore_signal(answer, inc=1, device_id=at_plane(sender), device_id_type=MESH)
+
+    def first_need(z, chunk):
+        for index, (source, step, _) in enumerate(ORDER[z]):
+            if (source == z and step >= chunk) or (source != z and chunk < CHUNKS):
                 return index
-        return len(ORDER[p])
-
-    def send_step(p, chunk):
-        for index in range(first_need(p, chunk), first_need(p, chunk + 1)):
-            source, step, _ = ORDER[p][index]
-            if source != p and all(item[:2] != (source, step) for item in ORDER[p][:index]):
-                wait_col(step, source)
-            line_copy(p, index).start()
+        return len(ORDER[z])
+
+    def send_step(z, chunk):
+        for index in range(first_need(z, chunk), first_need(z, chunk + 1)):
+            source, step, _ = ORDER[z][index]
+            if source != z and all(item[:2] != (source, step) for item in ORDER[z][:index]):
+                if source // N_ROW == z // N_ROW:
+                    wait_col(step, source % N_ROW)
+                else:
+                    wait_hop(step)
+            crossing = [i for i, item in enumerate(ORDER[z]) if item[2] // N_ROW != z // N_ROW]
+            if z < N_ROW and crossing and index == crossing[0]:
+                pl.semaphore_wait(answer, len([pair for pair in CROSSING if pair[0] == z]))
+            line_copy(z, index).start()
         if chunk == CHUNKS - 1:
-            relayed = [item[:2] for item in ORDER[p]]
-            for source in range(N_ROW):
+            relayed = [item[:2] for item in ORDER[z]]
+            for source in range(z // N_ROW * N_ROW, (z // N_ROW + 1) * N_ROW):
                 for step in range(CHUNKS):
-                    if source != p and (source, step) not in relayed:
-                        wait_col(step, source)
+                    if source != z and (source, step) not in relayed:
+                        wait_col(step, source % N_ROW)
 
     swaps, owns = [], []
 
@@ -228,12 +280,12 @@
         own = pltpu.make_async_copy(rows.at[c, chunk], cols.at[r, chunk], own_sem.at[chunk])
         own.start()
         owns.append(own)
-        each_place(lambda p: send_step(p, chunk))
+        each_plane(lambda z: send_step(z, chunk))
 
     for chunk in range(CHUNKS):
         channelise(chunk)
         if chunk == 0:
-            pl.semaphore_wait(barrier, GROUPS - 1 + 5)
+            each_plane(enter)
         turn(chunk)
         if chunk >= LAG:
             sends(chunk - LAG)
@@ -250,11 +302,11 @@
     for copy in swaps:
         copy.wait_send()
 
-    def finish(p):
-        for index in range(len(ORDER[p])):
-            line_copy(p, index).wait_send()
-
-    each_place(finish)
+    def finish(z):
+        for index in range(len(ORDER[z])):
+            line_copy(z, index).wait_send()
+
+    each_plane(finish)
     for chunk in range(CHUNKS):
         wait_row(chunk, hi * 2 + other)
         wait_row(chunk, (1 - hi) * 2 + other)
@@ -279,6 +331,7 @@
             pltpu.VMEM((WIDTH * ANT, 128), jnp.float32),
             pltpu.VMEM((BAND * ANT, 2 * WIDTH), jnp.float32),
             pltpu.VMEM((CHUNKS, GROUPS, PER, ANT, 2 * WIDTH), jnp.bfloat16),
+            pltpu.VMEM((max(1, len(HOPS)), PER, GROUPS, ANT, 2 * WIDTH), jnp.bfloat16),
             pltpu.SemaphoreType.DMA((CHUNKS,)),
             pltpu.SemaphoreType.DMA((3,)),
             pltpu.SemaphoreType.DMA((CHUNKS,)),
@@ -288,6 +341,8 @@
             pltpu.SemaphoreType.DMA((CHUNKS, N_ROW)),
             pltpu.SemaphoreType.DMA((CHUNKS, N_ROW)),
             pltpu.SemaphoreType.DMA((CHUNKS, 2)),
+            pltpu.SemaphoreType.DMA((max(1, len(HOPS)),)),
+            pltpu.SemaphoreType.REGULAR,
         ],
         compiler_params=pltpu.CompilerParams(
             collective_id=0, has_side_effects=True, vmem_limit_bytes=40 * 1024 * 1024

time: 40.9 us -> 39.8 us (0.973)
  Pallas kernels: 40.7 us -> 39.6 us
    pallas_call x1, Pallas kernels: 38.3 us -> 37.2 us  [gather(): pl.pallas_call(gather_kernel, out_shape=(shape, shape), in_specs=[anywher...]
where the time goes in v4:
time: 39.8 us; the launch traced here: 39.6 us
  Pallas kernels  39.6 us (99%)
    pallas_call x1, Pallas kernels, gather(): pl.pallas_call(gather_kernel, out_shape=(shape, shape), in_specs=[anywher...  37.2 us
    pallas_call x1, Pallas kernels, power(): pl.pallas_call(power_kernel, out_shape=jax.ShapeDtypeStruct((2, PER, 512...  2.41 us

profile of v4, /device:TPU:1, one launch (start us, length us, event | category | flops | bytes accessed | tf_op | source)
XLA Modules:
  0.0 39.6 jit_solution(15770000175340626787)
XLA Ops:
  0.0 37.2 %gather.1 = (bf16[4,4,2,16,8,128]{5,4,3,2,1,0:T(8,128)(2,1)S(1)}, bf16[4,4,2,16,8,128]{5,4,3,2,1,0:T(8,128)(2,1)S(1)}) custom-call(bf16[2,259,8,1024]{3,2,1,0:T(8,128)(2,1)} %bitcast.4, f32[2,1024,128]{2,1,0:T(8,128)} %constant.2.clone.waves, f32[4,1024]{1,0:T(4,128)} %window.1, s32[8,256]{1,0:T(8,128)} %flags.1), custom_call_target="tpu_custom_call" | custom-call | tf_op jit(solution)/shard_map/gather/pallas_call | solution.py:319
  37.2 2.4 %power.1 = f32[2,2,2048,128]{3,2,1,0:T(8,128)} custom-call(bf16[4,4,2,16,8,128]{5,4,3,2,1,0:T(8,128)(2,1)S(1)} %get-tuple-element.7.rows, bf16[4,4,2,16,8,128]{5,4,3,2,1,0:T(8,128)(2,1)S(1)} %get-tuple-element.8.cols), custom_call_target="tpu_custom_call" | custom-call | tf_op jit(solution)/shard_map/power/pallas_call | solution.py:382

commit v5 on v4

--- a/solution.py
+++ b/solution.py
@@ -78,8 +78,28 @@
     return np.stack([np.concatenate([cos, -sin] * 2, 1), np.concatenate([sin, cos] * 2, 1)])
 
 
+def column_of(cols, ch):
+    return jnp.concatenate(
+        [cols[:, t, ch].reshape(N_ROW * GROUPS * ANT, 2 * WIDTH) for t in range(CHUNKS)], axis=1
+    )
+
+
+def left_of(rows, ch, slot):
+    here = [rows[slot, t, ch].reshape(GROUPS * ANT, 2 * WIDTH) for t in range(CHUNKS)]
+    turned = [jnp.concatenate([x[:, WIDTH:], -x[:, :WIDTH]], axis=1) for x in here]
+    return jnp.concatenate([jnp.concatenate(here, axis=1), jnp.concatenate(turned, axis=1)], axis=0)
+
+
+def fill(out, left, column):
+    power = lax.dot_general(left, column, (((1,), (1,)), ((), ())), preferred_element_type=jnp.float32)
+    power = power * (1.0 / math.sqrt(SPECTRA))
+    for part in range(2):
+        for g in range(N_ROW):
+            out[part, pl.ds(g, 128, stride=N_ROW), :] = power[part * 128 : (part + 1) * 128, g * 128 : (g + 1) * 128]
+
+
 def gather_kernel(
-    volt, waves, window, flags, rows, cols,
+    volt, waves, window, flags, rows, cols, near,
     vbuf, wbuf, fbuf, kbuf, table, gbuf, cbuf, tbuf, sbuf, hop,
     volt_sem, small_sem, turn_send, turn_recv, own_sem, line_send, row_recv, col_recv, swap_send, hop_recv, answer,
 ):
@@ -291,11 +311,18 @@
             sends(chunk - LAG)
     for chunk in range(CHUNKS - LAG, CHUNKS):
         sends(chunk)
-    for chunk in range(CHUNKS):
+    for copy in owns:
+        copy.wait()
+    for chunk in range(CHUNKS):
+        wait_row(chunk, hi * 2 + other)
+    for chunk in range(CHUNKS):
+        if chunk >= CHUNKS - PER:
+            ch = chunk - (CHUNKS - PER)
+            column = column_of(cols, ch)
+            for piece in range(PIECES // 2):
+                fill(near.at[ch, piece], left_of(rows, ch, hi * 2 + piece), column)
         wait_row(chunk, far)
         swaps.append(swap(chunk, far, 1))
-    for copy in owns:
-        copy.wait()
     for chunk in range(CHUNKS):
         sent = sbuf.at[chunk, pl.ds(0, GROUPS - 1)]
         pltpu.make_async_copy(sent, sent, turn_send.at[chunk]).wait()
@@ -308,7 +335,6 @@
 
     each_plane(finish)
     for chunk in range(CHUNKS):
-        wait_row(chunk, hi * 2 + other)
         wait_row(chunk, (1 - hi) * 2 + other)
 
 
@@ -318,9 +344,9 @@
     inside = pl.BlockSpec(memory_space=pltpu.VMEM)
     return pl.pallas_call(
         gather_kernel,
-        out_shape=(shape, shape),
+        out_shape=(shape, shape, jax.ShapeDtypeStruct((PER, PIECES // 2, 2, 128 * N_ROW, 128), jnp.float32)),
         in_specs=[anywhere] * 4,
-        out_specs=(inside, inside),
+        out_specs=(inside, inside, inside),
         scratch_shapes=[
             pltpu.VMEM((2, PADDED, ANT, CHANNELS), jnp.bfloat16),
             pltpu.VMEM((2, CHANNELS, 128), jnp.float32),
@@ -351,52 +377,50 @@
     )(*(pltpu.with_memory_space_constraint(x, pltpu.HBM) for x in (volt, jnp.asarray(basis()), window, flags)))
 
 
-def power_kernel(rows, cols, out, held, sem):
-    side = 512 // PIECES
+def power_kernel(rows, cols, near, out, held, near_sem, sem):
+    hi = lax.axis_index("col") // 2
     copies = []
+
+    def write(src, ch, slot, where):
+        lines = pl.ds(pl.multiple_of(slot * 128 * N_ROW, 128 * N_ROW), 128 * N_ROW)
+        copy = pltpu.make_async_copy(src, out.at[:, ch, lines], where)
+        copy.start()
+        copies.append(copy)
+
     for ch in range(PER):
-        row, col = (
-            [ref[:, t, ch].reshape(N_ROW * GROUPS * ANT, 2 * WIDTH) for t in range(CHUNKS)] for ref in (rows, cols)
-        )
-        column = jnp.concatenate(col, axis=1)
-        for piece in range(PIECES):
-            here = [x[piece * side : (piece + 1) * side] for x in row]
-            turned = [jnp.concatenate([x[:, WIDTH:], -x[:, :WIDTH]], axis=1) for x in here]
-            left = jnp.concatenate([jnp.concatenate(here, axis=1), jnp.concatenate(turned, axis=1)], axis=0)
-            power = lax.dot_general(left, column, (((1,), (1,)), ((), ())), preferred_element_type=jnp.float32)
-            power = power * (1.0 / math.sqrt(SPECTRA))
-            for part in range(2):
-                for g in range(N_ROW):
-                    block = power[part * side : (part + 1) * side, g * 128 : (g + 1) * 128]
-                    held[ch, piece, part, pl.ds(g, side, stride=N_ROW), :] = block
-            lines = pl.ds(piece * side * N_ROW, side * N_ROW)
-            copy = pltpu.make_async_copy(held.at[ch, piece], out.at[:, ch, lines], sem.at[ch, piece])
-            copy.start()
-            copies.append(copy)
+        for piece in range(PIECES // 2):
+            write(near.at[ch, piece], ch, hi * 2 + piece, near_sem.at[ch, piece])
+    for ch in range(PER):
+        column = column_of(cols, ch)
+        for piece in range(PIECES // 2):
+            slot = (1 - hi) * 2 + piece
+            fill(held.at[ch, piece], left_of(rows, ch, slot), column)
+            write(held.at[ch, piece], ch, slot, sem.at[ch, piece])
     for copy in copies:
         copy.wait()
 
 
-def power(rows, cols):
+def power(rows, cols, near):
     inside = pl.BlockSpec(memory_space=pltpu.VMEM)
     return pl.pallas_call(
         power_kernel,
         out_shape=jax.ShapeDtypeStruct((2, PER, 512 * N_ROW, 128), jnp.float32),
-        in_specs=[inside, inside],
+        in_specs=[inside, inside, inside],
         out_specs=pl.BlockSpec(memory_space=pltpu.HBM),
         scratch_shapes=[
-            pltpu.VMEM((PER, PIECES, 2, 512 * N_ROW // PIECES, 128), jnp.float32),
-            pltpu.SemaphoreType.DMA((PER, PIECES)),
+            pltpu.VMEM((PER, PIECES // 2, 2, 128 * N_ROW, 128), jnp.float32),
+            pltpu.SemaphoreType.DMA((PER, PIECES // 2)),
+            pltpu.SemaphoreType.DMA((PER, PIECES // 2)),
         ],
         compiler_params=pltpu.CompilerParams(vmem_limit_bytes=40 * 1024 * 1024),
         name="power",
-    )(rows, cols)
+    )(rows, cols, near)
 
 
 def on_device(voltages, fir_window, flags):
     frames = voltages.reshape(2, ANT, FRAMES, CHANNELS).transpose(0, 2, 1, 3)
-    rows, cols = gather(frames, fir_window, flags)
-    return power(rows, cols).reshape(2, PER, 512, N_ROW, 128)
+    rows, cols, near = gather(frames, fir_window, flags)
+    return power(rows, cols, near).reshape(2, PER, 512, N_ROW, 128)
 
 
 def solution(mesh):

time: 39.8 us -> 39.9 us (level)
  no operation moved by 1% of the time
where the time goes in v5:
time: 39.9 us; the launch traced here: 39.7 us
  Pallas kernels  39.7 us (99%)
    pallas_call x1, Pallas kernels, gather(): pl.pallas_call(gather_kernel, out_shape=(shape, shape, jax.ShapeDtypeStru...  37.6 us
    pallas_call x1, Pallas kernels, power(): pl.pallas_call(power_kernel, out_shape=jax.ShapeDtypeStruct((2, PER, 512...  2.09 us

profile of v5, /device:TPU:1, one launch (start us, length us, event | category | flops | bytes accessed | tf_op | source)
XLA Modules:
  0.0 39.7 jit_solution(15213007203063129026)
XLA Ops:
  0.0 37.6 %gather.1 = (bf16[4,4,2,16,8,128]{5,4,3,2,1,0:T(8,128)(2,1)S(1)}, bf16[4,4,2,16,8,128]{5,4,3,2,1,0:T(8,128)(2,1)S(1)}, f32[2,2,2,512,128]{4,3,2,1,0:T(8,128)S(1)}) custom-call(bf16[2,259,8,1024]{3,2,1,0:T(8,128)(2,1)} %bitcast.4, f32[2,1024,128]{2,1,0:T(8,128)} %constant.2.clone.waves, f32[4,1024]{1,0:T(4,128)} %window.1, s32[8,256]{1,0:T(8,128)} %flags.1), custom_call_target="tpu_custom_call" | custom-call | tf_op jit(solution)/shard_map/gather/pallas_call | solution.py:345
  37.6 2.1 %power.1 = f32[2,2,2048,128]{3,2,1,0:T(8,128)} custom-call(bf16[4,4,2,16,8,128]{5,4,3,2,1,0:T(8,128)(2,1)S(1)} %get-tuple-element.8.rows, bf16[4,4,2,16,8,128]{5,4,3,2,1,0:T(8,128)(2,1)S(1)} %get-tuple-element.9.cols, f32[2,2,2,512,128]{4,3,2,1,0:T(8,128)S(1)} %get-tuple-element.10.near), custom_call_target="tpu_custom_call" | custom-call | tf_op jit(solution)/shard_map/power/pallas_call | solution.py:405

commit v6 on v5

--- a/solution.py
+++ b/solution.py
@@ -316,8 +316,8 @@
     for chunk in range(CHUNKS):
         wait_row(chunk, hi * 2 + other)
     for chunk in range(CHUNKS):
-        if chunk >= CHUNKS - PER:
-            ch = chunk - (CHUNKS - PER)
+        if chunk < PER:
+            ch = chunk
             column = column_of(cols, ch)
             for piece in range(PIECES // 2):
                 fill(near.at[ch, piece], left_of(rows, ch, hi * 2 + piece), column)

time: 39.9 us -> 39.5 us (0.990)
  Pallas kernels: 39.7 us -> 39.3 us
where the time goes in v6:
time: 39.5 us; the launch traced here: 39.3 us
  Pallas kernels  39.3 us (99%)
    pallas_call x1, Pallas kernels, gather(): pl.pallas_call(gather_kernel, out_shape=(shape, shape, jax.ShapeDtypeStru...  37.2 us
    pallas_call x1, Pallas kernels, power(): pl.pallas_call(power_kernel, out_shape=jax.ShapeDtypeStruct((2, PER, 512...  2.09 us

profile of v6, /device:TPU:1, one launch (start us, length us, event | category | flops | bytes accessed | tf_op | source)
XLA Modules:
  0.0 39.3 jit_solution(2622189556164361474)
XLA Ops:
  0.0 37.2 %gather.1 = (bf16[4,4,2,16,8,128]{5,4,3,2,1,0:T(8,128)(2,1)S(1)}, bf16[4,4,2,16,8,128]{5,4,3,2,1,0:T(8,128)(2,1)S(1)}, f32[2,2,2,512,128]{4,3,2,1,0:T(8,128)S(1)}) custom-call(bf16[2,259,8,1024]{3,2,1,0:T(8,128)(2,1)} %bitcast.4, f32[2,1024,128]{2,1,0:T(8,128)} %constant.2.clone.waves, f32[4,1024]{1,0:T(4,128)} %window.1, s32[8,256]{1,0:T(8,128)} %flags.1), custom_call_target="tpu_custom_call" | custom-call | tf_op jit(solution)/shard_map/gather/pallas_call | solution.py:345
  37.2 2.1 %power.1 = f32[2,2,2048,128]{3,2,1,0:T(8,128)} custom-call(bf16[4,4,2,16,8,128]{5,4,3,2,1,0:T(8,128)(2,1)S(1)} %get-tuple-element.8.rows, bf16[4,4,2,16,8,128]{5,4,3,2,1,0:T(8,128)(2,1)S(1)} %get-tuple-element.9.cols, f32[2,2,2,512,128]{4,3,2,1,0:T(8,128)S(1)} %get-tuple-element.10.near), custom_call_target="tpu_custom_call" | custom-call | tf_op jit(solution)/shard_map/power/pallas_call | solution.py:405

commit v7 on v6

--- a/solution.py
+++ b/solution.py
@@ -296,11 +296,15 @@
 
     def sends(chunk):
         turned(chunk)
+        last = chunk == CHUNKS - 1
+        if not last:
+            each_plane(lambda z: send_step(z, chunk))
         swaps.append(swap(chunk, c, 0))
         own = pltpu.make_async_copy(rows.at[c, chunk], cols.at[r, chunk], own_sem.at[chunk])
         own.start()
         owns.append(own)
-        each_plane(lambda z: send_step(z, chunk))
+        if last:
+            each_plane(lambda z: send_step(z, chunk))
 
     for chunk in range(CHUNKS):
         channelise(chunk)

time: 39.5 us -> 39.4 us (level)
  no operation moved by 1% of the time
where the time goes in v7:
time: 39.4 us; the launch traced here: 39.2 us
  Pallas kernels  39.2 us (99%)
    pallas_call x1, Pallas kernels, gather(): pl.pallas_call(gather_kernel, out_shape=(shape, shape, jax.ShapeDtypeStru...  37.1 us
    pallas_call x1, Pallas kernels, power(): pl.pallas_call(power_kernel, out_shape=jax.ShapeDtypeStruct((2, PER, 512...  2.09 us

profile of v7, /device:TPU:1, one launch (start us, length us, event | category | flops | bytes accessed | tf_op | source)
XLA Modules:
  0.0 39.2 jit_solution(16362065345737691309)
XLA Ops:
  0.0 37.1 %gather.1 = (bf16[4,4,2,16,8,128]{5,4,3,2,1,0:T(8,128)(2,1)S(1)}, bf16[4,4,2,16,8,128]{5,4,3,2,1,0:T(8,128)(2,1)S(1)}, f32[2,2,2,512,128]{4,3,2,1,0:T(8,128)S(1)}) custom-call(bf16[2,259,8,1024]{3,2,1,0:T(8,128)(2,1)} %bitcast.4, f32[2,1024,128]{2,1,0:T(8,128)} %constant.2.clone.waves, f32[4,1024]{1,0:T(4,128)} %window.1, s32[8,256]{1,0:T(8,128)} %flags.1), custom_call_target="tpu_custom_call" | custom-call | tf_op jit(solution)/shard_map/gather/pallas_call | solution.py:349
  37.1 2.1 %power.1 = f32[2,2,2048,128]{3,2,1,0:T(8,128)} custom-call(bf16[4,4,2,16,8,128]{5,4,3,2,1,0:T(8,128)(2,1)S(1)} %get-tuple-element.8.rows, bf16[4,4,2,16,8,128]{5,4,3,2,1,0:T(8,128)(2,1)S(1)} %get-tuple-element.9.cols, f32[2,2,2,512,128]{4,3,2,1,0:T(8,128)S(1)} %get-tuple-element.10.near), custom_call_target="tpu_custom_call" | custom-call | tf_op jit(solution)/shard_map/power/pallas_call | solution.py:409
